TPU v7x, 32 devices: a whole 2x2x4 slice. The times are simulated.
32 devices in a mesh: groups: 2 (over y), tensor: 4 (over z), adapter: 2 (over x), dp: 2 (over core).
Axes of the slice: x: 2, y: 2, z: 4, core: 2. Of those that a mesh axis runs over, the one named last changes fastest.
Arguments:
- tokens: bfloat16 [1024, 8192], P(('groups', 'adapter', 'dp'), 'tensor'), parts along dimension 0, may hold values from -6 to 6
- base_projection_weight: bfloat16 [8192, 2048], P(None, 'tensor'), may hold values from -0.0625 to 0.0625
- adapter_down_weight: bfloat16 [4, 8192, 64], P('adapter', 'tensor'), may hold values from -0.0625 to 0.0625
- adapter_up_weight: bfloat16 [4, 64, 2048], P('adapter', None, 'tensor'), may hold values from -0.75 to 0.75
- token_row_adapter: int32 [1024, 1], P(('groups', 'adapter', 'dp')), parts along dimension 0, may hold values from 0 to 3; in each aligned block of 128 rows (0 to 127, 128 to 255, ...) at most 128 rows name the same one
- adapter_slot_table: int32 [4], replicated, may hold values from 0 to 3, each once
Outputs:
- key_value: bfloat16 [1024, 2048], P(('groups', 'adapter', 'dp'), 'tensor'), parts along dimension 0
There are 2 independent parts, one for each index of `groups`. A program takes and returns all parts, laid end to end along the dimension named above; an argument that names none is the same for every part. Nothing has to cross between parts.
Inputs may be any that keep to these rules, and one draw needn't show every extreme that they name: `token_row_adapter`: among the 128 rows of one index of adapter+dp, no adapter id is named by more than 128 rows; in some of these blocks one is named by exactly 128; every id is named somewhere. `adapter_slot_table`: each slot once; slot s is stored on index s // 2 of adapter.
All inputs are finite; a program needn't handle non-finite values.
Results may differ from a plain program's by a relative error of at most 0.0035.
Values may be sent and summed in bfloat16 or wider, within the bound.
A program may use at most 64 MiB of HBM per device.

v0:
```python
import jax
import jax.numpy as jnp
from jax import lax
from jax.sharding import PartitionSpec as P

CAP = 128


adapter_scale = 0.5


def on_device(
    tokens,
    base_projection_weight,
    adapter_down_weight,
    adapter_up_weight,
    token_row_adapter,
    adapter_slot_table,
):
    feature_cols = tokens.shape[1]
    out_cols = base_projection_weight.shape[1]
    local_slot_list = adapter_down_weight.shape[0]
    adapter_count = adapter_slot_table.shape[0]
    owners = adapter_count // local_slot_list
    base_out = jnp.dot(
        lax.all_gather(tokens, "tensor", axis=1, tiled=True),
        base_projection_weight,
        preferred_element_type=jnp.float32,
    )
    adapter_ids = token_row_adapter[:, 0]
    onehot = (adapter_ids[:, None] == jnp.arange(adapter_count, dtype=jnp.int32)[None, :]).astype(
        jnp.int32
    )
    owner_slot = jnp.sum(onehot * adapter_slot_table[None, :], axis=1)
    position = jnp.sum((jnp.cumsum(onehot, axis=0) - 1) * onehot, axis=1)
    send_rows = (
        jnp.zeros((adapter_count, CAP, feature_cols), jnp.bfloat16)
        .at[owner_slot, position]
        .set(tokens)
    )
    grouped = send_rows.reshape(owners, local_slot_list, CAP, feature_cols)
    partial_value = jnp.einsum(
        "skcf,kfr->skcr",
        lax.all_to_all(grouped, "adapter", split_axis=0, concat_axis=0, tiled=True),
        adapter_down_weight,
        preferred_element_type=jnp.float32,
    )
    shrink_input = lax.psum(partial_value, "tensor").astype(jnp.bfloat16)
    expand_rows = jnp.einsum(
        "wvfx,vxg->wvfg", shrink_input, adapter_up_weight, preferred_element_type=jnp.float32
    )
    adapter_update = (adapter_scale * expand_rows).astype(jnp.bfloat16)
    returned = lax.all_to_all(adapter_update, "adapter", split_axis=0, concat_axis=0, tiled=True)
    flat_delta = returned.reshape(adapter_count * CAP, out_cols)
    row_delta = flat_delta[owner_slot * CAP + position]
    return (base_out + row_delta.astype(jnp.float32)).astype(jnp.bfloat16)


def solution(mesh):
    in_specs = (
        P(("groups", "adapter", "dp"), "tensor"),
        P(None, "tensor"),
        P("adapter", "tensor", None),
        P("adapter", None, "tensor"),
        P(("groups", "adapter", "dp"), None),
        P(),
    )
    out_specs = P(("groups", "adapter", "dp"), "tensor")
    return jax.shard_map(
        on_device, mesh=mesh, in_specs=in_specs, out_specs=out_specs, check_vma=False
    )
```

profile of v0, /device:TPU:0, one launch (start us, length us, event | category | flops | bytes accessed | tf_op | source)
XLA Modules:
  0.0 98.0 jit_solution(11121134321940062318)
XLA Ops:
  6.5 0.0 copy-start
  6.5 0.0 copy-start.1
  6.5 0.0 all-gather.2.cloned.1.call-start
  6.5 0.7 all-gather.2.cloned.1.call-update
  7.3 0.7 fusion.11
  8.0 0.2 reduce_window_sum.11
  8.2 0.8 select_reduce_fusion.1
  9.0 0.2 broadcast_in_dim.2
  9.3 0.0 copy-done.1
  9.3 12.2 %scatter_fusion = bf16[4,128,2048]{2,1,0:T(8,128)(2,1)S(1)} fusion(bf16[4,128,2048]{2,1,0:T(8,128)(2,1)S(1)} %broadcast_in_dim.2, s32[128]{0:T(128)S(1)} %get-tuple-element.8, bf16[128,2048]{1,0:T(8,128)(2,1)S(1)} %copy-done.1), kind=kCustom, calls=%fused_computation.1 | custom fusion | bytes 1573888 | tf_op jit(solution)/shard_map/scatter | solution.py:39
  21.5 28.8 %all_to_all.10 = bf16[2,2,128,2048]{3,2,1,0:T(8,128)(2,1)S(1)} all-to-all(bf16[2,2,128,2048]{3,2,1,0:T(8,128)(2,1)S(1)} %bitcast.38), channel_id=1, replica_groups=mesh['groups'=2,'tensor'=4,'adapter'=2,'dp'=2] {'adapter'}, dimensions={0} | all-to-all | bytes 4194304 | tf_op jit(solution)/shard_map/all_to_all | solution.py:44
  50.4 0.0 copy-done
  50.4 0.0 copy-start.2
  50.4 0.8 fusion.5
  51.1 21.9 %all-reduce.1 = bf16[2,2,128,64]{2,3,0,1:T(8,128)(2,1)S(1)} all-reduce(f32[2,2,128,64]{2,3,0,1:T(8,128)S(1)} %fusion.5), channel_id=1, replica_groups=mesh['groups'=2,'tensor'=4,'adapter'=2,'dp'=2] {'tensor'}, use_global_device_ids=true, to_apply=%region_4.5 | all-reduce | flops 32768 | bytes 196608 | tf_op jit(solution)/shard_map/psum | solution.py:48
  73.1 0.0 copy-done.2
  73.1 0.3 fusion.3
  73.4 0.8 copy.12
  74.2 3.5 %all-to-all-start.1 = ((bf16[2,2,128,512]{3,2,1,0:T(8,128)(2,1)}), bf16[2,2,128,512]{3,2,1,0:T(8,128)(2,1)S(1)}, u32[]{:S(2)}, u32[]{:S(2)}) async-start(bf16[2,2,128,512]{3,2,1,0:T(8,128)(2,1)} %copy.12), calls=%async_computation.1 | async-start | bytes 1048576 | tf_op jit(solution)/shard_map/all_to_all | solution.py:53
  77.7 6.5 %all-to-all-done.1 = bf16[2,2,128,512]{3,2,1,0:T(8,128)(2,1)S(1)} async-done(((bf16[2,2,128,512]{3,2,1,0:T(8,128)(2,1)}), bf16[2,2,128,512]{3,2,1,0:T(8,128)(2,1)S(1)}, u32[]{:S(2)}, u32[]{:S(2)}) %all-to-all-start.1) | async-done | bytes 524320 | tf_op jit(solution)/shard_map/all_to_all | solution.py:53
  84.3 0.8 gather_fusion
  85.1 0.0 all-gather.2.cloned.1.call-done
  85.2 5.9 %fusion.4 = bf16[128,512]{1,0:T(8,128)(2,1)} fusion(bf16[128,8192]{1,0:T(8,128)(2,1)} %all-gather.2.cloned.1.call-done, bf16[8192,512]{1,0:T(8,128)(2,1)} %param.7, bf16[128,512]{1,0:T(8,128)(2,1)S(1)} %gather_fusion), kind=kOutput, calls=%fused_computation.8 | convolution fusion | flops 1073938432 | bytes 10747904 | tf_op jit(solution)/shard_map/dot_general | solution.py:25
  (2 shorter events, 0.0 us)
Async XLA Ops:
  6.5 43.8 %copy-start = (bf16[2,2048,64]{1,2,0:T(8,128)(2,1)S(1)}, bf16[2,2048,64]{1,2,0:T(8,128)(2,1)}, u32[]{:S(2)}) copy-start(bf16[2,2048,64]{1,2,0:T(8,128)(2,1)} %param.8) | copy-start | bytes 1572868
  6.5 2.8 %copy-start.1 = (bf16[128,2048]{1,0:T(8,128)(2,1)S(1)}, bf16[128,2048]{1,0:T(8,128)(2,1)}, u32[]{:S(2)}) copy-start(bf16[128,2048]{1,0:T(8,128)(2,1)} %param.6) | copy-start | bytes 1572868
  6.5 78.6 %all-gather.2.cloned.1.call-start = ((), (), s32[]{:S(2)}) async-start(), calls=%async_computation.2 | async-start | bytes 2621440 | tf_op jit(solution)/shard_map/all_gather | solution.py:26
  50.4 22.7 %copy-start.2 = (bf16[2,64,512]{2,1,0:T(8,128)(2,1)S(1)}, bf16[2,64,512]{2,1,0:T(8,128)(2,1)}, u32[]{:S(2)}) copy-start(bf16[2,64,512]{2,1,0:T(8,128)(2,1)} %param.9) | copy-start | bytes 393220
  74.2 10.1 %all-to-all-start.1 = ((bf16[2,2,128,512]{3,2,1,0:T(8,128)(2,1)}), bf16[2,2,128,512]{3,2,1,0:T(8,128)(2,1)S(1)}, u32[]{:S(2)}, u32[]{:S(2)}) async-start(bf16[2,2,128,512]{3,2,1,0:T(8,128)(2,1)} %copy.12), calls=%async_computation.1 | async-start | bytes 1048576 | tf_op jit(solution)/shard_map/all_to_all | solution.py:53
Sparse Core Ops, SparseCore 0:
  8.9 49.2 all-gather.1
where the time goes:
time: 98.2 us; the launch traced here: 98 us
  blocking collectives  50.7 us (52%)
  local copies, waits for them, and re-layouts  14.2 us (14%)
  between operations  13.5 us (14%)
  waiting for transfers between devices  7.28 us (7%)
  matrix products  7.04 us (7%)
  starting transfers between devices  3.49 us (4%)
  other arithmetic  1.77 us (2%)
    all_to_all x1, blocking collectives, on_device(): lax.all_to_all(grouped, 'adapter', split_axis=0, concat_axis=0, tiled=True)  28.8 us
    psum x1, blocking collectives, on_device(): shrink_input = lax.psum(partial_value, 'tensor').astype(jnp.bfloat16)  21.9 us
    scatter x1, local copies, waits for them, and re-layouts, on_device(): send_rows = jnp.zeros((adapter_count, CAP, feature_cols), jnp.bfloat16).a...  12.2 us
    all_to_all x1, waiting for transfers between devices, on_device(): lax.all_to_all(adapter_update, 'adapter', split_axis=0, concat_axis=0, ti...  6.55 us
    dot_general x1, matrix products, on_device(): jnp.dot(lax.all_gather(tokens, 'tensor', axis=1, tiled=True), base_projec...  5.94 us
    all_to_all x1, starting transfers between devices, on_device(): lax.all_to_all(adapter_update, 'adapter', split_axis=0, concat_axis=0, ti...  3.49 us
  transfers between devices with their start and end apart: 2, of which 1 were waited for; matrix products, arithmetic and copies ran while one was open for 17% of the time, Pallas kernels for 0%

commit v1 on v0

v1 whole, which is shorter than its diff:
```python
import functools

import jax
import jax.numpy as jnp
from jax import lax
from jax.experimental import pallas as pl
from jax.experimental.pallas import tpu as pltpu
from jax.sharding import PartitionSpec as P

MESH = pl.DeviceIdType.MESH
CHUNKS = 4
adapter_scale = 0.5


def kernel(
    n,
    owners,
    ids_ref,
    table_ref,
    tok_ref,
    w_ref,
    down_ref,
    up_ref,
    out_ref,
    got,
    wv,
    dv,
    uv,
    part,
    acc,
    tok_sem,
    w_sem,
    own_sem,
    right_sem,
    left_sem,
    got_sem,
    xs_sem,
    xr_sem,
    ps_sem,
    pr_sem,
):
    z = lax.axis_index("tensor")
    x = lax.axis_index("adapter")
    rows, feats = tok_ref.shape
    width = feats // CHUNKS
    slots, rank, _ = down_ref.shape
    total_slots = owners * slots

    barrier = pltpu.get_barrier_semaphore()
    for d in range(1, n):
        pl.semaphore_signal(
            barrier, inc=1, device_id={"tensor": lax.rem(z + d, n)}, device_id_type=MESH
        )
    for d in range(1, owners):
        pl.semaphore_signal(
            barrier, inc=1, device_id={"adapter": lax.rem(x + d, owners)}, device_id_type=MESH
        )

    tok_copies = []
    for c in range(CHUNKS):
        cp = pltpu.make_async_copy(
            tok_ref.at[:, pl.ds(c * width, width)], got.at[z, c], tok_sem.at[c]
        )
        cp.start()
        tok_copies.append(cp)

    def w_copy(k):
        return pltpu.make_async_copy(
            w_ref.at[pl.ds(pl.multiple_of(k * feats, feats), feats), :], wv.at[k], w_sem.at[k]
        )

    for d in range(n):
        w_copy(lax.rem(z + d, n)).start()
    own_down = pltpu.make_async_copy(down_ref, dv.at[x], own_sem.at[0])
    own_up = pltpu.make_async_copy(up_ref, uv.at[x], own_sem.at[1])
    own_down.start()
    own_up.start()

    pl.semaphore_wait(barrier, n - 1 + owners - 1)

    def send(src, shard, c, to_right):
        return pltpu.make_async_remote_copy(
            src_ref=src,
            dst_ref=got.at[shard, c],
            send_sem=(right_sem if to_right else left_sem).at[shard, c],
            recv_sem=got_sem.at[shard, c],
            device_id={"tensor": z + 1 if to_right else z - 1},
            device_id_type=MESH,
        )

    def own_send(c, to_right):
        return send(tok_ref.at[:, pl.ds(c * width, width)], z, c, to_right)

    def forward(shard, c, to_right):
        return send(got.at[shard, c], shard, c, to_right)

    for c in range(CHUNKS):

        @pl.when(z < n - 1)
        def _():
            own_send(c, True).start()

        @pl.when(z > 0)
        def _():
            own_send(c, False).start()

    def weight_copies(d):
        to = lax.rem(x + d, owners)
        return [
            pltpu.make_async_remote_copy(
                src_ref=src,
                dst_ref=dst.at[x],
                send_sem=xs_sem.at[k, to],
                recv_sem=xr_sem.at[k, x],
                device_id={"adapter": to},
                device_id_type=MESH,
            )
            for k, (src, dst) in enumerate(((down_ref, dv), (up_ref, uv)))
        ]

    for d in range(1, owners):
        for cp in weight_copies(d):
            cp.start()

    def mul(shard, c):
        acc[...] += jnp.dot(
            got[shard, c],
            wv[shard, pl.ds(c * width, width), :],
            preferred_element_type=jnp.float32,
        )

    acc[...] = jnp.zeros_like(acc)
    w_copy(z).wait()
    for c in range(CHUNKS):
        tok_copies[c].wait()
        mul(z, c)
    for d in range(1, n):
        w_copy(lax.rem(z + d, n)).wait()

    def step(t):
        low, high = z - t, z + t
        for c in range(CHUNKS):

            @pl.when(low >= 0)
            def _():
                forward(low, c, True).wait_recv()

                @pl.when(z < n - 1)
                def _():
                    forward(low, c, True).start()

            @pl.when(high < n)
            def _():
                forward(high, c, False).wait_recv()

                @pl.when(z > 0)
                def _():
                    forward(high, c, False).start()

            @pl.when(low >= 0)
            def _():
                mul(low, c)

            @pl.when(high < n)
            def _():
                mul(high, c)

    slot = jnp.zeros(ids_ref.shape, jnp.int32)
    for g in range(total_slots):
        slot = slot + jnp.where(ids_ref[...] == g, table_ref[g], 0)

    def part_copy(d):
        to = lax.rem(z + d, n)
        return pltpu.make_async_remote_copy(
            src_ref=part.at[z],
            dst_ref=part.at[z],
            send_sem=ps_sem.at[to],
            recv_sem=pr_sem.at[z],
            device_id={"tensor": to},
            device_id_type=MESH,
        )

    def arrived(ref, sem):
        pltpu.make_async_copy(ref, ref, sem).wait()

    step(1)

    own_down.wait()
    own_up.wait()
    for d in range(1, owners):
        src = lax.rem(x + d, owners)
        arrived(dv.at[src], xr_sem.at[0, src])
        arrived(uv.at[src], xr_sem.at[1, src])
    own_part = jnp.zeros((rank, rows), jnp.float32)
    for o in range(owners):
        down = dv[o].reshape(slots * rank, feats)
        prod = jnp.zeros((slots * rank, rows), jnp.float32)
        for c in range(CHUNKS):
            prod = prod + lax.dot_general(
                down[:, c * width : (c + 1) * width],
                got[z, c],
                (((1,), (1,)), ((), ())),
                preferred_element_type=jnp.float32,
            )
        for s in range(slots):
            own_part = own_part + jnp.where(
                slot == o * slots + s, prod[s * rank : (s + 1) * rank], 0.0
            )
    part[z] = own_part
    for d in range(1, n):
        part_copy(d).start()

    def middle(t, carry):
        step(t)
        return carry

    lax.fori_loop(2, n - 1, middle, 0)

    for d in range(1, n):
        src = lax.rem(z + d, n)
        arrived(part.at[src], pr_sem.at[src])
    shrink = part[0]
    for k in range(1, n):
        shrink = shrink + part[k]
    shrink = shrink.astype(jnp.bfloat16).astype(jnp.float32)
    spread = jnp.concatenate(
        [jnp.where(slot == k, shrink, 0.0) for k in range(total_slots)], axis=0
    ).astype(jnp.bfloat16)
    delta = lax.dot_general(
        spread,
        uv[...].reshape(total_slots * rank, uv.shape[-1]),
        (((0,), (0,)), ((), ())),
        preferred_element_type=jnp.float32,
    )
    acc[...] += (adapter_scale * delta).astype(jnp.bfloat16).astype(jnp.float32)

    step(n - 1)
    out_ref[...] = acc[...].astype(jnp.bfloat16)

    for c in range(CHUNKS):

        @pl.when(z < n - 1)
        def _():
            own_send(c, True).wait_send()

        @pl.when(z > 0)
        def _():
            own_send(c, False).wait_send()

    def drain(t, carry):
        for c in range(CHUNKS):

            @pl.when(jnp.logical_and(z - t >= 0, z < n - 1))
            def _():
                forward(z - t, c, True).wait_send()

            @pl.when(jnp.logical_and(z + t < n, z > 0))
            def _():
                forward(z + t, c, False).wait_send()

        return carry

    lax.fori_loop(1, n, drain, 0)
    for d in range(1, owners):
        for cp in weight_copies(d):
            cp.wait_send()
    for d in range(1, n):
        part_copy(d).wait_send()


def on_device(
    n,
    owners,
    tokens,
    base_projection_weight,
    adapter_down_weight,
    adapter_up_weight,
    token_row_adapter,
    adapter_slot_table,
):
    rows, feats = tokens.shape
    out_cols = base_projection_weight.shape[1]
    slots, _, rank = adapter_down_weight.shape
    width = feats // CHUNKS
    any_spec = pl.BlockSpec(memory_space=pl.ANY)
    dma = pltpu.SemaphoreType.DMA
    bf16 = jnp.bfloat16
    return pl.pallas_call(
        functools.partial(kernel, n, owners),
        out_shape=jax.ShapeDtypeStruct((rows, out_cols), bf16),
        in_specs=[
            pl.BlockSpec(memory_space=pltpu.VMEM),
            pl.BlockSpec(memory_space=pltpu.SMEM),
            any_spec,
            any_spec,
            any_spec,
            any_spec,
        ],
        out_specs=pl.BlockSpec(memory_space=pltpu.VMEM),
        scratch_shapes=[
            pltpu.VMEM((n, CHUNKS, rows, width), bf16),
            pltpu.VMEM((n, feats, out_cols), bf16),
            pltpu.VMEM((owners, slots, rank, feats), bf16),
            pltpu.VMEM((owners, slots, rank, out_cols), bf16),
            pltpu.VMEM((n, rank, rows), jnp.float32),
            pltpu.VMEM((rows, out_cols), jnp.float32),
            dma((CHUNKS,)),
            dma((n,)),
            dma((2,)),
            dma((n, CHUNKS)),
            dma((n, CHUNKS)),
            dma((n, CHUNKS)),
            dma((2, owners)),
            dma((2, owners)),
            dma((n,)),
            dma((n,)),
        ],
        compiler_params=pltpu.CompilerParams(
            collective_id=0, has_side_effects=True, vmem_limit_bytes=60 * 1024 * 1024
        ),
    )(
        token_row_adapter.T,
        adapter_slot_table,
        tokens,
        base_projection_weight,
        jnp.swapaxes(adapter_down_weight, 1, 2),
        adapter_up_weight,
    )


def solution(mesh):
    in_specs = (
        P(("groups", "adapter", "dp"), "tensor"),
        P(None, "tensor"),
        P("adapter", "tensor", None),
        P("adapter", None, "tensor"),
        P(("groups", "adapter", "dp"), None),
        P(),
    )
    out_specs = P(("groups", "adapter", "dp"), "tensor")
    return jax.shard_map(
        functools.partial(on_device, mesh.shape["tensor"], mesh.shape["adapter"]),
        mesh=mesh,
        in_specs=in_specs,
        out_specs=out_specs,
        check_vma=False,
    )
```

time: 98.2 us -> 46.2 us (0.47)
  blocking collectives: 50.7 us -> 0 us
  Pallas kernels: 0 us -> 44.5 us
  between operations: 13.5 us -> 0.01 us
  local copies, waits for them, and re-layouts: 14.2 us -> 1.57 us
  waiting for transfers between devices: 7.28 us -> 0 us
  matrix products: 7.04 us -> 0 us
  starting transfers between devices: 3.49 us -> 0 us
  other arithmetic: 1.77 us -> 0 us
    pallas_call x0 -> x1, Pallas kernels: none -> 44.5 us  [on_device(): pl.pallas_call(functools.partial(kernel, n, owners), out_shape=jax.ShapeD...]
    all_to_all x1 -> x0, blocking collectives: 28.8 us -> none  [on_device(): lax.all_to_all(grouped, 'adapter', split_axis=0, concat_axis=0, tiled=True)]
    psum x1 -> x0, blocking collectives: 21.9 us -> none  [on_device(): shrink_input = lax.psum(partial_value, 'tensor').astype(jnp.bfloat16)]
    scatter x1 -> x0, local copies, waits for them, and re-layouts: 12.2 us -> none  [on_device(): send_rows = jnp.zeros((adapter_count, CAP, feature_cols), jnp.bfloat16).a...]
    dot_general x3 -> x0, matrix products: 7.04 us -> none  [the longest x1 5.94 us: on_device(): jnp.dot(lax.all_gather(tokens, 'tensor', axis=1, tiled=True), base_projec...]
    all_to_all x1 -> x0, waiting for transfers between devices: 6.55 us -> none  [on_device(): lax.all_to_all(adapter_update, 'adapter', split_axis=0, concat_axis=0, ti...]
    all_to_all x1 -> x0, starting transfers between devices: 3.49 us -> none  [on_device(): lax.all_to_all(adapter_update, 'adapter', split_axis=0, concat_axis=0, ti...]
    unnamed x6 -> x1, local copies, waits for them, and re-layouts: 0.01 us -> 1.57 us
  transfers between devices with their start and end apart: 2 -> 0, of which waited for: 1 -> 0; matrix products, arithmetic and copies ran while one was open for 17% -> 0% of each run, Pallas kernels for 0% -> 0%
where the time goes in v1:
time: 46.2 us; the launch traced here: 46.1 us
  Pallas kernels  44.5 us (96%)
  local copies, waits for them, and re-layouts  1.57 us (3%)
    pallas_call x1, Pallas kernels, on_device(): pl.pallas_call(functools.partial(kernel, n, owners), out_shape=jax.ShapeD...  44.5 us
    unnamed x1, local copies, waits for them, and re-layouts  1.57 us

profile of v1, /device:TPU:0, one launch (start us, length us, event | category | flops | bytes accessed | tf_op | source)
XLA Modules:
  0.0 46.1 jit_solution(8808352437801254440)
XLA Ops:
  0.0 44.5 %shard_map.64 = bf16[128,512]{1,0:T(8,128)(2,1)} custom-call(s32[1,128]{1,0:T(1,128)} %bitcast.3, s32[4]{0:T(128)} %table_ref.1, bf16[128,2048]{1,0:T(8,128)(2,1)} %tok_ref.1, bf16[8192,512]{1,0:T(8,128)(2,1)} %w_ref.1, bf16[2,64,2048]{2,1,0:T(8,128)(2,1)} %bitcast.2, bf16[2,64,512]{2,1,0:T(8,128)(2,1)} %up_ref.1), custom_call_target="tpu_custom_call" | custom-call | tf_op jit(solution)/shard_map/pallas_call | solution.py:288
  44.5 1.6 %copy.8 = bf16[128,512]{1,0:T(8,128)(2,1)} copy(bf16[128,512]{1,0:T(8,128)(2,1)} %shard_map.64) | data formatting | bytes 262144

commit v2 on v1

v2 whole, which is shorter than its diff:
```python
import functools

import jax
import jax.numpy as jnp
from jax import lax
from jax.experimental import pallas as pl
from jax.experimental.pallas import tpu as pltpu
from jax.sharding import PartitionSpec as P

MESH = pl.DeviceIdType.MESH
MOST_CHUNKS = 8
LANES = 128
LAG = 2
adapter_scale = 0.5


def kernel(
    n,
    owners,
    ids_ref,
    table_ref,
    tok_ref,
    w_ref,
    down_ref,
    up_ref,
    out_ref,
    got,
    wv,
    wx,
    dv,
    uv,
    part,
    pout,
    pin,
    acc,
    tok_sem,
    w_sem,
    own_sem,
    right_sem,
    left_sem,
    got_sem,
    ws_sem,
    wy_sem,
    wc_sem,
    wr_sem,
    po_sem,
    xs_sem,
    xr_sem,
    ps_sem,
    pr_sem,
):
    z = lax.axis_index("tensor")
    x = lax.axis_index("adapter")
    y = lax.axis_index("groups")
    core = lax.axis_index("dp")
    rows, feats = tok_ref.shape
    chunks = got.shape[1]
    width = feats // chunks
    slots, rank, _ = down_ref.shape
    total_slots = owners * slots
    quarter = feats // 4
    piece = quarter // chunks

    is_end = jnp.logical_or(z == 0, z == n - 1)
    is_relay = jnp.logical_or(z == 1, z == n - 2)
    relay = jnp.where(z == 0, 1, n - 2)
    end = jnp.where(z == 1, 0, n - 1)

    barrier = pltpu.get_barrier_semaphore()
    peers = [{"tensor": lax.rem(z + d, n)} for d in range(1, n)]
    peers += [{"adapter": lax.rem(x + d, owners)} for d in range(1, owners)]
    peers += [{"groups": 1 - y}, {"dp": 1 - core}]
    for peer in peers:
        pl.semaphore_signal(barrier, inc=1, device_id=peer, device_id_type=MESH)

    tok_copies = []
    for c in range(chunks):
        cp = pltpu.make_async_copy(
            tok_ref.at[:, pl.ds(c * width, width)], got.at[z, c], tok_sem.at[c]
        )
        cp.start()
        tok_copies.append(cp)

    def w_copy(k):
        return pltpu.make_async_copy(
            w_ref.at[pl.ds(pl.multiple_of(k * feats, feats), feats), :], wv.at[k], w_sem.at[k]
        )

    w_copy(z).start()
    pl.semaphore_wait(barrier, len(peers))

    def remote(src, dst, send_sem, recv_sem, to):
        return pltpu.make_async_remote_copy(
            src_ref=src,
            dst_ref=dst,
            send_sem=send_sem,
            recv_sem=recv_sem,
            device_id=to,
            device_id_type=MESH,
        )

    def arrived(ref, sem):
        pltpu.make_async_copy(ref, ref, sem).wait()

    def send(src, shard, c, to_right):
        return remote(
            src,
            got.at[shard, c],
            (right_sem if to_right else left_sem).at[shard, c],
            got_sem.at[shard, c],
            {"tensor": z + 1 if to_right else z - 1},
        )

    def own_send(c, to_right):
        return send(tok_ref.at[:, pl.ds(c * width, width)], z, c, to_right)

    def forward(shard, c, to_right):
        return send(got.at[shard, c], shard, c, to_right)

    inner_right = jnp.logical_and(z > 0, z < n - 2)
    inner_left = jnp.logical_and(z < n - 1, z > 1)

    mine = 2 * y + core
    across = 2 * (1 - y) + core

    def w_piece(q, i):
        return wx.at[q, pl.ds(i * piece, piece), :]

    def w_send(i):
        start = relay * feats + mine * quarter + i * piece
        src = w_ref.at[pl.ds(pl.multiple_of(start, piece), piece), :]
        return remote(
            src, w_piece(mine, i), ws_sem.at[i], wr_sem.at[mine, i], {"tensor": relay}
        )

    def w_across(i):
        src = w_piece(mine, i)
        return remote(src, src, wy_sem.at[i], wr_sem.at[mine, i], {"groups": 1 - y})

    def w_core(q, i):
        src = w_piece(q, i)
        return remote(
            src, src, wc_sem.at[(q - core) // 2, i], wr_sem.at[q, i], {"dp": 1 - core}
        )

    @pl.when(is_end)
    def _():
        for c in range(chunks):
            w_send(c).start()

    for c in range(chunks):

        @pl.when(inner_right)
        def _():
            own_send(c, True).start()

        @pl.when(inner_left)
        def _():
            own_send(c, False).start()

    def weight_copies(d):
        to = lax.rem(x + d, owners)
        return [
            remote(src, dst.at[x], xs_sem.at[k, to], xr_sem.at[k, x], {"adapter": to})
            for k, (src, dst) in enumerate(((down_ref, dv), (up_ref, uv)))
        ]

    for d in range(1, owners):
        for cp in weight_copies(d):
            cp.start()
    own_down = pltpu.make_async_copy(down_ref, dv.at[x], own_sem.at[0])
    own_up = pltpu.make_async_copy(up_ref, uv.at[x], own_sem.at[1])
    own_down.start()
    own_up.start()
    for d in range(1, n):
        w_copy(lax.rem(z + d, n)).start()

    def mul(shard, c):
        acc[...] += jnp.dot(
            got[shard, c],
            wv[shard, pl.ds(c * width, width), :],
            preferred_element_type=jnp.float32,
        )

    def sources(t):
        low = z - t - jnp.where(z == n - 1, 1, 0) + jnp.where(z == 1, 1, 0)
        high = z + t + jnp.where(z == 0, 1, 0) - jnp.where(z == n - 2, 1, 0)
        return low, high, jnp.logical_and(low >= 0, low < z), jnp.logical_and(high < n, high > z)

    def take_low(low, c):
        arrived(got.at[low, c], got_sem.at[low, c])

        @pl.when(z < n - 1)
        def _():
            forward(low, c, True).start()

    def step(t, hook=None, before=None):
        low, high, has_low, has_high = sources(t)
        left_half = z < n // 2
        for c in range(chunks):

            @pl.when(jnp.logical_and(has_low, left_half))
            def _():
                take_low(low, c)

            @pl.when(has_high)
            def _():
                arrived(got.at[high, c], got_sem.at[high, c])

                @pl.when(z > 0)
                def _():
                    forward(high, c, False).start()

            @pl.when(jnp.logical_and(has_low, jnp.logical_not(left_half)))
            def _():
                take_low(low, c)

            if before is not None:
                before(c)

            @pl.when(has_low)
            def _():
                mul(low, c)

            @pl.when(has_high)
            def _():
                mul(high, c)

            if hook is not None:
                hook(c)

    slot = jnp.zeros(ids_ref.shape, jnp.int32)
    for g in range(total_slots):
        slot = slot + jnp.where(ids_ref[...] == g, table_ref[g], 0)

    def part_copy(d):
        to = lax.rem(z + d, n)
        return remote(part.at[z], part.at[z], ps_sem.at[to], pr_sem.at[z], {"tensor": to})

    def own_work():
        acc[...] = jnp.zeros_like(acc)
        w_copy(z).wait()
        for c in range(chunks):
            tok_copies[c].wait()
            mul(z, c)
        for d in range(1, n):
            w_copy(lax.rem(z + d, n)).wait()

    def relay_piece(i):
        arrived(w_piece(mine, i), wr_sem.at[mine, i])
        w_across(i).start()
        w_core(mine, i).start()

    def relay_across(i):
        arrived(w_piece(across, i), wr_sem.at[across, i])
        w_core(across, i).start()

    def first_before(c):
        @pl.when(is_relay)
        def _():
            relay_piece(c)
            if c >= LAG:
                relay_across(c - LAG)

        if c >= chunks - 3:
            at = 2 * (c - chunks + 3)
            to = at + 2 if c < chunks - 1 else chunks

            @pl.when(is_end)
            def _():
                for i in range(at, to):

                    @pl.when(z == 0)
                    def _():
                        own_send(i, True).start()

                    @pl.when(z == n - 1)
                    def _():
                        own_send(i, False).start()

    def second_before(c):
        if c < LAG:

            @pl.when(is_relay)
            def _():
                relay_across(chunks - LAG + c)

    def relay_product():
        other = 1 - core
        for i in range(chunks):
            arrived(w_piece(other, i), wr_sem.at[other, i])
            arrived(w_piece(2 + other, i), wr_sem.at[2 + other, i])
        total = jnp.zeros(acc.shape, jnp.float32)
        per = chunks // 4
        for c in range(chunks):
            total = total + jnp.dot(
                got[z, c],
                wx[c // per, (c % per) * width : (c % per + 1) * width, :],
                preferred_element_type=jnp.float32,
            )
        pout[...] = total.astype(jnp.bfloat16)
        product_copy().start()

    def product_copy():
        return remote(pout, pin, po_sem.at[0], po_sem.at[1], {"tensor": end})

    def shrink_part():
        own_down.wait()
        own_up.wait()
        for d in range(1, owners):
            src = lax.rem(x + d, owners)
            arrived(dv.at[src], xr_sem.at[0, src])
            arrived(uv.at[src], xr_sem.at[1, src])
        own_part = jnp.zeros((rank, rows), jnp.float32)
        for o in range(owners):
            down = dv[o].reshape(slots * rank, feats)
            prod = jnp.zeros((slots * rank, rows), jnp.float32)
            for c in range(chunks):
                prod = prod + lax.dot_general(
                    down[:, c * width : (c + 1) * width],
                    got[z, c],
                    (((1,), (1,)), ((), ())),
                    preferred_element_type=jnp.float32,
                )
            for s in range(slots):
                own_part = own_part + jnp.where(
                    slot == o * slots + s, prod[s * rank : (s + 1) * rank], 0.0
                )
        part[z] = own_part
        for d in range(1, n):
            part_copy(d).start()

    def expand():
        for d in range(1, n):
            src = lax.rem(z + d, n)
            arrived(part.at[src], pr_sem.at[src])
        shrink = part[0]
        for k in range(1, n):
            shrink = shrink + part[k]
        shrink = shrink.astype(jnp.bfloat16).astype(jnp.float32)
        spread = jnp.concatenate(
            [jnp.where(slot == k, shrink, 0.0) for k in range(total_slots)], axis=0
        ).astype(jnp.bfloat16)
        delta = lax.dot_general(
            spread,
            uv[...].reshape(total_slots * rank, uv.shape[-1]),
            (((0,), (0,)), ((), ())),
            preferred_element_type=jnp.float32,
        )
        acc[...] += (adapter_scale * delta).astype(jnp.bfloat16).astype(jnp.float32)

    def second_hook(c):
        if c == 1:
            shrink_part()
        if c == 3:

            @pl.when(is_relay)
            def _():
                relay_product()

        if c == chunks - 2:
            expand()
        if c == max(chunks - 2, 3):

            @pl.when(is_end)
            def _():
                arrived(pin, po_sem.at[1])
                acc[...] += pin[...].astype(jnp.float32)

    own_work()
    step(1, before=first_before)
    step(2, hook=second_hook, before=second_before)

    def later(t, carry):
        step(t)
        return carry

    lax.fori_loop(3, n - 1, later, 0)
    out_ref[...] = acc[...].astype(jnp.bfloat16)

    for c in range(chunks):

        @pl.when(z < n - 2)
        def _():
            own_send(c, True).wait_send()

        @pl.when(z > 1)
        def _():
            own_send(c, False).wait_send()

        @pl.when(is_end)
        def _():
            w_send(c).wait_send()

        @pl.when(is_relay)
        def _():
            w_across(c).wait_send()
            w_core(mine, c).wait_send()
            w_core(across, c).wait_send()

    @pl.when(is_relay)
    def _():
        product_copy().wait_send()

    def drain(t, carry):
        low, high, has_low, has_high = sources(t)
        for c in range(chunks):

            @pl.when(jnp.logical_and(has_low, z < n - 1))
            def _():
                forward(low, c, True).wait_send()

            @pl.when(jnp.logical_and(has_high, z > 0))
            def _():
                forward(high, c, False).wait_send()

        return carry

    lax.fori_loop(1, n - 1, drain, 0)
    for d in range(1, owners):
        for cp in weight_copies(d):
            cp.wait_send()
    for d in range(1, n):
        part_copy(d).wait_send()


def on_device(
    n,
    owners,
    tokens,
    base_projection_weight,
    adapter_down_weight,
    adapter_up_weight,
    token_row_adapter,
    adapter_slot_table,
):
    rows, feats = tokens.shape
    out_cols = base_projection_weight.shape[1]
    slots, _, rank = adapter_down_weight.shape
    chunks = min(MOST_CHUNKS, feats // LANES)
    width = feats // chunks
    any_spec = pl.BlockSpec(memory_space=pl.ANY)
    dma = pltpu.SemaphoreType.DMA
    bf16 = jnp.bfloat16
    return pl.pallas_call(
        functools.partial(kernel, n, owners),
        out_shape=jax.ShapeDtypeStruct((rows, out_cols), bf16),
        in_specs=[
            pl.BlockSpec(memory_space=pltpu.VMEM),
            pl.BlockSpec(memory_space=pltpu.SMEM),
            any_spec,
            any_spec,
            any_spec,
            any_spec,
        ],
        out_specs=pl.BlockSpec(memory_space=pltpu.VMEM),
        scratch_shapes=[
            pltpu.VMEM((n, chunks, rows, width), bf16),
            pltpu.VMEM((n, feats, out_cols), bf16),
            pltpu.VMEM((4, feats // 4, out_cols), bf16),
            pltpu.VMEM((owners, slots, rank, feats), bf16),
            pltpu.VMEM((owners, slots, rank, out_cols), bf16),
            pltpu.VMEM((n, rank, rows), jnp.float32),
            pltpu.VMEM((rows, out_cols), bf16),
            pltpu.VMEM((rows, out_cols), bf16),
            pltpu.VMEM((rows, out_cols), jnp.float32),
            dma((chunks,)),
            dma((n,)),
            dma((2,)),
            dma((n, chunks)),
            dma((n, chunks)),
            dma((n, chunks)),
            dma((chunks,)),
            dma((chunks,)),
            dma((2, chunks)),
            dma((4, chunks)),
            dma((2,)),
            dma((2, owners)),
            dma((2, owners)),
            dma((n,)),
            dma((n,)),
        ],
        compiler_params=pltpu.CompilerParams(
            collective_id=0, has_side_effects=True, vmem_limit_bytes=60 * 1024 * 1024
        ),
    )(
        token_row_adapter.T,
        adapter_slot_table,
        tokens,
        base_projection_weight,
        jnp.swapaxes(adapter_down_weight, 1, 2),
        adapter_up_weight,
    )


def solution(mesh):
    in_specs = (
        P(("groups", "adapter", "dp"), "tensor"),
        P(None, "tensor"),
        P("adapter", "tensor", None),
        P("adapter", None, "tensor"),
        P(("groups", "adapter", "dp"), None),
        P(),
    )
    out_specs = P(("groups", "adapter", "dp"), "tensor")
    return jax.shard_map(
        functools.partial(on_device, mesh.shape["tensor"], mesh.shape["adapter"]),
        mesh=mesh,
        in_specs=in_specs,
        out_specs=out_specs,
        check_vma=False,
    )
```

time: 46.2 us -> 65.5 us (1.42)
  Pallas kernels: 44.5 us -> 63.7 us
    pallas_call x1, Pallas kernels: 44.5 us -> 63.7 us  [on_device(): pl.pallas_call(functools.partial(kernel, n, owners), out_shape=jax.ShapeD...]
where the time goes in v2:
time: 65.5 us; the launch traced here: 65.3 us
  Pallas kernels  63.7 us (97%)
  local copies, waits for them, and re-layouts  1.57 us (2%)
    pallas_call x1, Pallas kernels, on_device(): pl.pallas_call(functools.partial(kernel, n, owners), out_shape=jax.ShapeD...  63.7 us
    unnamed x1, local copies, waits for them, and re-layouts  1.57 us

profile of v2, /device:TPU:0, one launch (start us, length us, event | category | flops | bytes accessed | tf_op | source)
XLA Modules:
  0.0 65.3 jit_solution(7973898158739668422)
XLA Ops:
  0.0 63.7 %shard_map.64 = bf16[128,512]{1,0:T(8,128)(2,1)} custom-call(s32[1,128]{1,0:T(1,128)} %bitcast.3, s32[4]{0:T(128)} %table_ref.1, bf16[128,2048]{1,0:T(8,128)(2,1)} %tok_ref.1, bf16[8192,512]{1,0:T(8,128)(2,1)} %w_ref.1, bf16[2,64,2048]{2,1,0:T(8,128)(2,1)} %bitcast.2, bf16[2,64,512]{2,1,0:T(8,128)(2,1)} %up_ref.1), custom_call_target="tpu_custom_call" | custom-call | tf_op jit(solution)/shard_map/pallas_call | solution.py:445
  63.7 1.6 %copy.8 = bf16[128,512]{1,0:T(8,128)(2,1)} copy(bf16[128,512]{1,0:T(8,128)(2,1)} %shard_map.64) | data formatting | bytes 262144

commit v3 on v1

--- a/solution.py
+++ b/solution.py
@@ -206,7 +206,7 @@
             own_part = own_part + jnp.where(
                 slot == o * slots + s, prod[s * rank : (s + 1) * rank], 0.0
             )
-    part[z] = own_part
+    part[z] = own_part.astype(jnp.bfloat16)
     for d in range(1, n):
         part_copy(d).start()
 
@@ -219,9 +219,9 @@
     for d in range(1, n):
         src = lax.rem(z + d, n)
         arrived(part.at[src], pr_sem.at[src])
-    shrink = part[0]
+    shrink = part[0].astype(jnp.float32)
     for k in range(1, n):
-        shrink = shrink + part[k]
+        shrink = shrink + part[k].astype(jnp.float32)
     shrink = shrink.astype(jnp.bfloat16).astype(jnp.float32)
     spread = jnp.concatenate(
         [jnp.where(slot == k, shrink, 0.0) for k in range(total_slots)], axis=0
@@ -302,7 +302,7 @@
             pltpu.VMEM((n, feats, out_cols), bf16),
             pltpu.VMEM((owners, slots, rank, feats), bf16),
             pltpu.VMEM((owners, slots, rank, out_cols), bf16),
-            pltpu.VMEM((n, rank, rows), jnp.float32),
+            pltpu.VMEM((n, rank, rows), bf16),
             pltpu.VMEM((rows, out_cols), jnp.float32),
             dma((CHUNKS,)),
             dma((n,)),

time: 46.2 us -> 45.2 us (0.978)
  Pallas kernels: 44.5 us -> 43.5 us
    pallas_call x1, Pallas kernels: 44.5 us -> 43.5 us  [on_device(): pl.pallas_call(functools.partial(kernel, n, owners), out_shape=jax.ShapeD...]
where the time goes in v3:
time: 45.2 us; the launch traced here: 45 us
  Pallas kernels  43.5 us (96%)
  local copies, waits for them, and re-layouts  1.57 us (3%)
    pallas_call x1, Pallas kernels, on_device(): pl.pallas_call(functools.partial(kernel, n, owners), out_shape=jax.ShapeD...  43.5 us
    unnamed x1, local copies, waits for them, and re-layouts  1.57 us

profile of v3, /device:TPU:0, one launch (start us, length us, event | category | flops | bytes accessed | tf_op | source)
XLA Modules:
  0.0 45.0 jit_solution(16985960591695377931)
XLA Ops:
  0.0 43.5 %shard_map.64 = bf16[128,512]{1,0:T(8,128)(2,1)} custom-call(s32[1,128]{1,0:T(1,128)} %bitcast.3, s32[4]{0:T(128)} %table_ref.1, bf16[128,2048]{1,0:T(8,128)(2,1)} %tok_ref.1, bf16[8192,512]{1,0:T(8,128)(2,1)} %w_ref.1, bf16[2,64,2048]{2,1,0:T(8,128)(2,1)} %bitcast.2, bf16[2,64,512]{2,1,0:T(8,128)(2,1)} %up_ref.1), custom_call_target="tpu_custom_call" | custom-call | tf_op jit(solution)/shard_map/pallas_call | solution.py:288
  43.5 1.6 %copy.8 = bf16[128,512]{1,0:T(8,128)(2,1)} copy(bf16[128,512]{1,0:T(8,128)(2,1)} %shard_map.64) | data formatting | bytes 262144
